TPU v7x, 128 devices: a whole 4x4x4 slice. The times are simulated.
128 devices in a mesh: sample: 16 (over z_hi, x, core), tensor: 8 (over z_lo, y).
Axes of the slice: x: 4, y: 4, z: 4 (z_hi: 2, z_lo: 2; z = z_hi * 2 + z_lo), core: 2. Of those that a mesh axis runs over, the one named last changes fastest.
Arguments:
- stepwise_feed_vectors: bfloat16 [4, 64, 8192], P(None, 'sample'), may hold values from -6 to 6
- prelude_rescaling_factor: bfloat16 [8192], replicated, may hold values from 0.099609375 to 1.8984375
- probe_mapping_matrix: bfloat16 [8192, 8, 1024], P('sample', 'tensor'), may hold values from -0.125 to 0.125
- paired_mapping_matrix: bfloat16 [8192, 8, 256], P('sample', 'tensor'), may hold values from -0.0625 to 0.0625
- final_mapping_matrix: bfloat16 [8192, 8, 1024], P('sample', 'tensor'), may hold values from -0.1875 to 0.1875
- memory_pair_tensor: bfloat16 [256, 8, 2, 512, 128], P('sample', 'tensor'), may hold values from -240 to 240, as said below
- retained_draw_ids: int32 [64], replicated, may hold values from 0 to 255, as said below
- valid_extents: int32 [256], replicated, may hold values from 64 to 512, as said below
Outputs:
- attn_out: bfloat16 [4, 64, 8192], P(None, 'sample', 'tensor')
Inputs may be any that keep to these rules, and one draw needn't show every extreme that they name: `retained_draw_ids`: 64 distinct sampled rows; surviving rows g * 16 to (g + 1) * 16 - 1 form group g. Within one group at most 2 survivors lie in one aligned block of 16 sampled rows, and in every group some block holds exactly 2. `valid_extents`: some sampled rows of every draw use all 512 positions, among them a survivor of each group. `memory_pair_tensor`: keys and values of the sampled rows' caches.
All inputs are finite; a program needn't handle non-finite values.
Results may differ from a plain program's by a relative error of at most 0.02.
The roundings to bfloat16 on the way count: a program that leaves them out, or rounds other values in their place, can miss the bound.
Values may be sent and summed in bfloat16 or wider, within the bound.
No kernel may reach another device: no remote copies, remote signals or barrier semaphores. Data moves between devices by JAX's collectives and lax.ppermute only.
A program may use at most 128 MiB of HBM per device.

v0:
```python
import jax
import jax.numpy as jnp
from jax import lax
from jax.sharding import PartitionSpec as P

SURV_GRP = 16
CAP = 2


norm_eps = 1e-05


def from_partner(shard, axis, distance):
    return lax.ppermute(shard, axis, [(i, i ^ 1 << distance) for i in range(lax.axis_size(axis))])


def attend(query_vectors, memory_element_tally, latest_projection, valid_extent_bounds):
    key_rows = memory_element_tally[:, 0]
    cached_value_rows = memory_element_tally[:, 1]
    softmax_scale = query_vectors.shape[-1] ** (-0.5)
    cached_scores = (
        jnp.einsum("bsgd,bcd->bsgc", query_vectors, key_rows, preferred_element_type=jnp.float32)
        * softmax_scale
    )
    extent = key_rows.shape[1]
    cached_scores = jnp.where(
        jnp.arange(extent)[None, None, None, :] < valid_extent_bounds[:, None, None, None],
        cached_scores,
        -jnp.inf,
    )
    latest_token_scores = (
        jnp.einsum(
            "rauv,rnv->raun",
            query_vectors,
            latest_projection[:, :, 0],
            preferred_element_type=jnp.float32,
        )
        * softmax_scale
    )
    step_count = latest_projection.shape[1]
    causal = jnp.arange(step_count)[None, :] <= jnp.arange(step_count)[:, None]
    latest_token_scores = jnp.where(causal[None, :, None, :], latest_token_scores, -jnp.inf)
    highest = jnp.maximum(jnp.max(cached_scores, -1), jnp.max(latest_token_scores, -1))
    cached_probs = jnp.exp(cached_scores - highest[..., None])
    fresh_probs = jnp.exp(latest_token_scores - highest[..., None])
    totals = jnp.sum(cached_probs, -1) + jnp.sum(fresh_probs, -1)
    weighted_value_sum = jnp.einsum(
        "mijl,mlt->mijt",
        cached_probs.astype(jnp.bfloat16),
        cached_value_rows,
        preferred_element_type=jnp.float32,
    )
    weighted_value_sum = weighted_value_sum + jnp.einsum(
        "hiax,hxm->hiam",
        fresh_probs.astype(jnp.bfloat16),
        latest_projection[:, :, 1],
        preferred_element_type=jnp.float32,
    )
    result = (weighted_value_sum / totals[..., None]).astype(jnp.bfloat16)
    return result.reshape(result.shape[0], result.shape[1], result.shape[2] * result.shape[3])


def normalize(tokens, prelude_rescaling_factor):
    widened = tokens.astype(jnp.float32)
    return (
        widened
        * lax.rsqrt(jnp.mean(widened * widened, -1, keepdims=True) + norm_eps)
        * prelude_rescaling_factor.astype(jnp.float32)
    ).astype(jnp.bfloat16)


def per_device(
    stepwise_feed_vectors,
    prelude_rescaling_factor,
    probe_mapping_matrix,
    paired_mapping_matrix,
    final_mapping_matrix,
    memory_pair_tensor,
    retained_draw_ids,
    valid_extents,
):
    blocks = lax.axis_size("sample")
    groups = blocks // 4
    sample_index = lax.axis_index("sample")
    quarter = sample_index % 4
    my_group = sample_index // 4
    head_cols = probe_mapping_matrix.shape[2] // 4
    head_size = paired_mapping_matrix.shape[2] // 2
    local_heads = head_cols // head_size
    step_count = stepwise_feed_vectors.shape[0]
    model_width = stepwise_feed_vectors.shape[2]
    members = SURV_GRP

    def spread(shard_piece):
        return jnp.tile(shard_piece.reshape(shard_piece.shape[0], 4, head_cols), (1, groups, 1))

    tokens = stepwise_feed_vectors
    for which_bit in range(2):
        partner = from_partner(tokens, "sample", which_bit)
        upper_half = quarter // (1 << which_bit) % 2 == 1
        tokens = jnp.where(
            upper_half, jnp.concatenate([partner, tokens], 1), jnp.concatenate([tokens, partner], 1)
        )
    normed = normalize(tokens, prelude_rescaling_factor)
    flat_rows = normed.reshape(step_count * members, model_width)
    kv_copies = jnp.broadcast_to(
        paired_mapping_matrix,
        (paired_mapping_matrix.shape[0], blocks, paired_mapping_matrix.shape[2]),
    )
    query_all, kv_all, out_all = (
        lax.all_to_all(
            spread(probe_mapping_matrix), "sample", split_axis=1, concat_axis=0, tiled=True
        ),
        lax.all_to_all(kv_copies, "sample", split_axis=1, concat_axis=0, tiled=True),
        lax.all_to_all(
            spread(final_mapping_matrix), "sample", split_axis=1, concat_axis=0, tiled=True
        ),
    )
    query_mine = jnp.dot(
        flat_rows, query_all.reshape(model_width, head_cols), preferred_element_type=jnp.float32
    ).astype(jnp.bfloat16)
    fresh_rows = jnp.dot(
        flat_rows, kv_all.reshape(model_width, 2 * head_size), preferred_element_type=jnp.float32
    ).astype(jnp.bfloat16)
    query_mine = query_mine.reshape(step_count, members, head_cols)
    fresh_rows = fresh_rows.reshape(step_count, members, 2 * head_size)
    local_strand_total = memory_pair_tensor.shape[0]
    cache_len = memory_pair_tensor.shape[3]
    memory_element_tally = memory_pair_tensor.reshape(local_strand_total, 2, cache_len, head_size)
    parameter_tally_total = retained_draw_ids.shape[0]
    position = jnp.arange(parameter_tally_total)
    parent_strands = retained_draw_ids // local_strand_total
    group_of = position // members
    same_place = (parent_strands[:, None] == parent_strands[None, :]) & (
        group_of[:, None] == group_of[None, :]
    )
    slot_rank = jnp.sum(same_place & (position[None, :] < position[:, None]), axis=1)
    local_strand_ordinal = retained_draw_ids % local_strand_total
    strand_memory_extents = jnp.take(valid_extents, retained_draw_ids)
    owned_rows = (
        (parent_strands == sample_index)[:, None, None]
        & (group_of[:, None, None] == jnp.arange(groups)[None, :, None])
        & (slot_rank[:, None, None] == jnp.arange(CAP)[None, None, :])
    )
    send_rows = jnp.sum(jnp.where(owned_rows, local_strand_ordinal[:, None, None], 0), 0)
    my_source = lax.dynamic_slice_in_dim(parent_strands, my_group * members, members)
    my_slot = lax.dynamic_slice_in_dim(slot_rank, my_group * members, members)
    pick_rows = my_source * CAP + my_slot
    selected_rows = jnp.take(memory_element_tally, send_rows.reshape(-1), axis=0).reshape(
        groups, 1, CAP, 2, cache_len, head_size
    )
    outgoing = jnp.broadcast_to(selected_rows, (groups, 4, CAP, 2, cache_len, head_size)).reshape(
        blocks, CAP, 2, cache_len, head_size
    )
    arrived = lax.all_to_all(outgoing, "sample", split_axis=0, concat_axis=0, tiled=True)
    my_rows = jnp.take(arrived.reshape(blocks * CAP, 2, cache_len, head_size), pick_rows, axis=0)
    my_lengths = lax.dynamic_slice_in_dim(strand_memory_extents, my_group * members, members)
    query_vectors = query_mine.reshape(step_count, members, local_heads, head_size).transpose(
        1, 0, 2, 3
    )
    latest_projection = fresh_rows.reshape(step_count, members, 2, head_size).transpose(1, 0, 2, 3)
    answer = attend(query_vectors, my_rows, latest_projection, my_lengths)
    answer_rows = answer.reshape(members * step_count, head_cols)
    out_mine = out_all.reshape(model_width, head_cols)
    weighted_value_sum = lax.psum_scatter(
        lax.dot_general(
            out_mine, answer_rows, (((1,), (1,)), ((), ())), preferred_element_type=jnp.float32
        ).astype(jnp.bfloat16),
        "tensor",
        scatter_dimension=0,
        tiled=True,
    ).astype(jnp.float32)
    for which_bit in (1, 0):
        half_cols = weighted_value_sum.shape[1] // 2
        keep_half = quarter // (1 << which_bit) % 2
        kept_half = lax.dynamic_slice_in_dim(
            weighted_value_sum, keep_half * half_cols, half_cols, 1
        )
        other_half = lax.dynamic_slice_in_dim(
            weighted_value_sum, (1 - keep_half) * half_cols, half_cols, 1
        )
        weighted_value_sum = kept_half + from_partner(
            other_half.astype(jnp.bfloat16), "sample", which_bit
        ).astype(other_half.dtype)
    return (
        weighted_value_sum.reshape(weighted_value_sum.shape[0], members // 4, step_count)
        .transpose(2, 1, 0)
        .astype(jnp.bfloat16)
    )


def solution(mesh):
    placed = (
        P(None, "sample", None),
        P(),
        P("sample", "tensor", None),
        P("sample", "tensor", None),
        P("sample", "tensor", None),
        P("sample", "tensor", None, None, None),
        P(),
        P(),
    )
    return jax.shard_map(
        per_device,
        mesh=mesh,
        in_specs=placed,
        out_specs=P(None, "sample", "tensor"),
        check_vma=False,
    )
```

profile of v0, /device:TPU:24, one launch (start us, length us, event | category | flops | bytes accessed | tf_op | source)
XLA Modules:
  0.0 389.3 jit_solution(15995972304694577951)
XLA Ops:
  6.5 0.0 copy-start
  6.5 1.9 tile.20
  8.4 0.1 copy.21
  8.6 0.4 tile.21
  9.0 0.0 copy-start.3
  9.0 59.4 %all_to_all.50 = bf16[512,16,256]{2,0,1:T(8,128)(2,1)} all-to-all(bf16[512,16,256]{2,0,1:T(8,128)(2,1)S(1)} %bitcast.93), channel_id=1, replica_groups=mesh['sample'=16,'tensor'=8] {'sample'}, dimensions={1} | all-to-all | bytes 8388608 | tf_op jit(solution)/shard_map/all_to_all | solution.py:111
  68.4 0.0 copy-done.3
  68.4 2.3 broadcast_in_dim.114
  70.8 0.0 copy-start.6
  70.8 4.7 %all-to-all-start.2 = ((bf16[512,16,256]{2,0,1:T(8,128)(2,1)}), bf16[512,16,256]{2,0,1:T(8,128)(2,1)}, u32[]{:S(2)}, u32[]{:S(2)}) async-start(bf16[512,16,256]{2,0,1:T(8,128)(2,1)} %broadcast_in_dim.114), calls=%async_computation.2 | async-start | bytes 8388608 | tf_op jit(solution)/shard_map/all_to_all | solution.py:114
  75.5 0.0 copy-done.6
  75.5 0.0 copy-done
  75.5 0.8 gather_fusion
  76.3 0.2 convert_reduce_fusion
  76.5 0.1 select_reduce_fusion
  76.7 0.1 copy.24
  76.8 0.1 reshape.342
  76.9 0.1 copy.23
  77.0 4.3 %gather_fusion.1 = bf16[8,2,512,128]{3,2,1,0:T(8,128)(2,1)} fusion(bf16[16,2,512,128]{3,2,1,0:T(8,128)(2,1)} %bitcast.97, s32[1024]{0:T(1024)S(1)} %pad_clamp_fusion.1), kind=kCustom, calls=%fused_computation.1 | custom fusion | bytes 4194336 | tf_op jit(solution)/shard_map/jit(_take)/gather | solution.py:149
  81.3 1.9 broadcast_select_fusion
  83.2 48.5 %all-to-all-done.2 = bf16[512,16,256]{2,0,1:T(8,128)(2,1)} async-done(((bf16[512,16,256]{2,0,1:T(8,128)(2,1)}), bf16[512,16,256]{2,0,1:T(8,128)(2,1)}, u32[]{:S(2)}, u32[]{:S(2)}) %all-to-all-start.2) | async-done | bytes 4194336 | tf_op jit(solution)/shard_map/all_to_all | solution.py:114
  131.7 5.2 %broadcast_in_dim.108 = bf16[4,4,2,2,512,128]{5,4,3,2,1,0:T(8,128)(2,1)} broadcast(bf16[4,2,2,512,128]{4,3,2,1,0:T(8,128)(2,1)S(1)} %broadcast_select_fusion), dimensions={0,2,3,4,5} | broadcast | bytes 10485760 | tf_op jit(solution)/shard_map/broadcast_in_dim | solution.py:152
  136.9 6.4 %all-to-all-start.1 = ((bf16[16,2,2,512,128]{4,3,2,1,0:T(8,128)(2,1)}), bf16[16,2,2,512,128]{4,3,2,1,0:T(8,128)(2,1)}, u32[]{:S(2)}, u32[]{:S(2)}) async-start(bf16[16,2,2,512,128]{4,3,2,1,0:T(8,128)(2,1)} %bitcast.90), calls=%async_computation.1 | async-start | bytes 16777216 | tf_op jit(solution)/shard_map/all_to_all | solution.py:155
  143.4 0.0 copy-done.4
  143.4 0.4 collective-permute-start
  143.8 0.0 copy-done.5
  143.8 0.0 copy-done.2
  143.8 0.8 tile.23
  144.6 0.1 copy.29
  144.8 0.1 dynamic_slice.21
  144.8 0.6 collective-permute-done
  145.5 0.5 maximum_select_fusion.1
  146.0 1.8 collective-permute-start.1
  147.7 0.1 compare_and_fusion.1
  147.8 0.1 iota_compare_fusion.1
  147.9 119.6 %collective-permute-done.1 = bf16[4,8,8192]{2,1,0:T(8,128)(2,1)S(1)} collective-permute-done((bf16[4,8,8192]{2,1,0:T(8,128)(2,1)S(1)}, bf16[4,8,8192]{2,1,0:T(8,128)(2,1)S(1)}, u32[]{:S(2)}, u32[]{:S(2)}) %collective-permute-start.1) | collective-permute-done | bytes 524320 | tf_op jit(solution)/shard_map/ppermute | solution.py:14
  267.5 0.4 fusion.1
  267.9 0.0 all-to-all-done.1
  268.0 2.4 tile.24
  270.3 6.2 %all-to-all-start.3 = ((bf16[512,16,256]{2,0,1:T(8,128)(2,1)}), bf16[512,16,256]{2,0,1:T(8,128)(2,1)}, u32[]{:S(2)}, u32[]{:S(2)}) async-start(bf16[512,16,256]{2,0,1:T(8,128)(2,1)} %bitcast.92), calls=%async_computation.3 | async-start | bytes 8388608 | tf_op jit(solution)/shard_map/all_to_all | solution.py:115
  276.5 0.0 reduce-scatter.2.cloned.1.call-start
  276.5 0.3 fusion.3
  276.9 3.0 convolution_convert_fusion.2
  279.9 3.0 convolution_convert_fusion.1
  283.0 0.4 fusion.29
  283.4 6.4 %gather_fusion.2 = bf16[16,2,512,128]{3,2,1,0:T(8,128)(2,1)} fusion(bf16[32,2,512,128]{3,2,1,0:T(8,128)(2,1)} %bitcast.10, s32[1024]{0:T(1024)S(1)} %pad_clamp_fusion), kind=kCustom, calls=%fused_computation.2 | custom fusion | bytes 8388672 | tf_op jit(solution)/shard_map/jit(_take)/gather | solution.py:156
  289.8 2.6 copy_select_fusion
  292.4 0.8 fusion.28
  293.2 0.1 fusion.15
  293.3 0.2 fusion.11
  293.6 0.0 copy-start.1
  293.6 0.5 fusion.4
  294.1 0.2 fusion.10
  294.3 38.5 %all-to-all-done.3 = bf16[512,16,256]{2,0,1:T(8,128)(2,1)} async-done(((bf16[512,16,256]{2,0,1:T(8,128)(2,1)}), bf16[512,16,256]{2,0,1:T(8,128)(2,1)}, u32[]{:S(2)}, u32[]{:S(2)}) %all-to-all-start.3) | async-done | bytes 4194336 | tf_op jit(solution)/shard_map/all_to_all | solution.py:115
  332.8 4.5 %fusion = bf16[8192,64]{0,1:T(8,128)(2,1)} fusion(bf16[8192,256]{1,0:T(8,128)(2,1)} %bitcast.31, bf16[8,8,2,128]{3,2,1,0:T(2,128)(2,1)S(1)} %bitcast.99), kind=kOutput, calls=%fused_computation.4 | convolution fusion | flops 268959744 | bytes 5275648 | tf_op jit(solution)/shard_map/dot_general | solution.py:166
  337.4 0.0 reduce-scatter.2.cloned.1.call-update
  337.4 37.8 %reduce-scatter.2.cloned.1.call-done = bf16[1024,64]{0,1:T(8,128)(2,1)} async-done(((bf16[8192,64]{0,1:T(8,128)(2,1)}), bf16[1024,64]{0,1:T(8,128)(2,1)}) %reduce-scatter.2.cloned.1.call-update) | async-done | bytes 131088 | tf_op jit(solution)/shard_map/reduce_scatter | solution.py:165
  375.2 0.9 convert_element_type.95
  376.1 1.4 collective-permute-start.2
  377.6 2.9 collective-permute-done.2
  380.5 0.1 collective-permute-start.3
  380.6 1.2 collective-permute-done.3
  381.8 0.6 copy.56
  382.5 0.0 copy-done.1
  (27 shorter events, 0.3 us)
Async XLA Ops:
  6.5 69.0 %copy-start = (s32[256]{0:T(256)S(1)}, s32[256]{0:T(256)}, u32[]{:S(2)}) copy-start(s32[256]{0:T(256)} %param.15) | copy-start | bytes 3076
  9.0 59.5 %copy-start.3 = (bf16[512,1,256]{2,0,1:T(8,128)(2,1)S(1)}, bf16[512,1,256]{2,0,1:T(8,128)(2,1)}, u32[]{:S(2)}) copy-start(bf16[512,1,256]{2,0,1:T(8,128)(2,1)} %param.11) | copy-start | bytes 786436
  70.8 4.7 %copy-start.6 = (s32[64]{0:T(128)S(1)}, s32[64]{0:T(128)}, u32[]{:S(2)}) copy-start(s32[64]{0:T(128)} %param.14) | copy-start | bytes 772
  70.8 60.9 %all-to-all-start.2 = ((bf16[512,16,256]{2,0,1:T(8,128)(2,1)}), bf16[512,16,256]{2,0,1:T(8,128)(2,1)}, u32[]{:S(2)}, u32[]{:S(2)}) async-start(bf16[512,16,256]{2,0,1:T(8,128)(2,1)} %broadcast_in_dim.114), calls=%async_computation.2 | async-start | bytes 8388608 | tf_op jit(solution)/shard_map/all_to_all | solution.py:114
  136.9 6.4 %copy-start.4 = (bf16[4,4,8192]{2,1,0:T(4,128)(2,1)S(1)}, bf16[4,4,8192]{2,1,0:T(4,128)(2,1)}, u32[]{:S(2)}) copy-start(bf16[4,4,8192]{2,1,0:T(4,128)(2,1)} %param.8) | copy-start | bytes 786436
  136.9 6.9 %copy-start.5 = (bf16[8192]{0:T(1024)(128)(2,1)S(1)}, bf16[8192]{0:T(1024)(128)(2,1)}, u32[]{:S(2)}) copy-start(bf16[8192]{0:T(1024)(128)(2,1)} %param.9) | copy-start | bytes 49156
  136.9 6.9 %copy-start.2 = (bf16[512,1,1024]{2,0,1:T(8,128)(2,1)S(1)}, bf16[512,1,1024]{2,0,1:T(8,128)(2,1)}, u32[]{:S(2)}) copy-start(bf16[512,1,1024]{2,0,1:T(8,128)(2,1)} %param.12) | copy-start | bytes 3145732
  136.9 131.0 %all-to-all-start.1 = ((bf16[16,2,2,512,128]{4,3,2,1,0:T(8,128)(2,1)}), bf16[16,2,2,512,128]{4,3,2,1,0:T(8,128)(2,1)}, u32[]{:S(2)}, u32[]{:S(2)}) async-start(bf16[16,2,2,512,128]{4,3,2,1,0:T(8,128)(2,1)} %bitcast.90), calls=%async_computation.1 | async-start | bytes 16777216 | tf_op jit(solution)/shard_map/all_to_all | solution.py:155
  143.4 2.1 collective-permute-start
  146.0 121.5 %collective-permute-start.1 = (bf16[4,8,8192]{2,1,0:T(8,128)(2,1)S(1)}, bf16[4,8,8192]{2,1,0:T(8,128)(2,1)S(1)}, u32[]{:S(2)}, u32[]{:S(2)}) collective-permute-start(bf16[4,8,8192]{2,1,0:T(8,128)(2,1)S(1)} %maximum_select_fusion.1), channel_id=1, source_target_pairs={{0,16},{8,24},{16,0},{24,8},{32,48},{40,56},{48,32},{56,40},{64,80... | collective-permute-start | bytes 1572872 | tf_op jit(solution)/shard_map/ppermute | solution.py:14
  270.3 62.5 %all-to-all-start.3 = ((bf16[512,16,256]{2,0,1:T(8,128)(2,1)}), bf16[512,16,256]{2,0,1:T(8,128)(2,1)}, u32[]{:S(2)}, u32[]{:S(2)}) async-start(bf16[512,16,256]{2,0,1:T(8,128)(2,1)} %bitcast.92), calls=%async_computation.3 | async-start | bytes 8388608 | tf_op jit(solution)/shard_map/all_to_all | solution.py:115
  276.5 98.7 %reduce-scatter.2.cloned.1.call-start = ((), (), s32[]{:S(2)}) async-start(), calls=%async_computation.5 | async-start | bytes 1179648 | tf_op jit(solution)/shard_map/reduce_scatter | solution.py:165
  293.6 88.9 %copy-start.1 = (s32[256]{0:T(256)S(1)}, s32[256]{0:T(256)}, u32[]{:S(2)}) copy-start(s32[256]{0:T(256)} %param.15) | copy-start | bytes 3076
  376.1 4.3 %collective-permute-start.2 = (bf16[1024,32]{0,1:T(8,128)(2,1)S(1)}, bf16[1024,32]{0,1:T(8,128)(2,1)S(1)}, u32[]{:S(2)}, u32[]{:S(2)}) collective-permute-start(bf16[1024,32]{0,1:T(8,128)(2,1)S(1)} %dynamic-slice_convert_fusion), channel_id=1, source_target_pairs={{0,16},{8,24},{16,0},{24,8},{32,48},{40,56},{48,32},{56,40},{64,80... | collective-permute-start | bytes 196616 | tf_op jit(solution)/shard_map/ppermute | solution.py:14
  380.5 1.3 collective-permute-start.3
Sparse Core Ops, SparseCore 0:
  337.5 37.5 reduce-scatter.1
where the time goes:
time: 393 us; the launch traced here: 389 us
  waiting for transfers between devices  249 us (63%)
  blocking collectives  59.4 us (15%)
  local copies, waits for them, and re-layouts  26 us (7%)
  starting transfers between devices  21 us (5%)
  between operations  13.7 us (3%)
  matrix products  12.5 us (3%)
  other arithmetic  7.59 us (2%)
    ppermute x4, waiting for transfers between devices, from_partner(): lax.ppermute(shard, axis, [(i, i ^ 1 << distance) for i in range(lax.axis...  124 us
    all_to_all x1, blocking collectives, per_device(): lax.all_to_all(spread(probe_mapping_matrix), 'sample', split_axis=1, conc...  59.4 us
    all_to_all x1, waiting for transfers between devices, per_device(): lax.all_to_all(kv_copies, 'sample', split_axis=1, concat_axis=0, tiled=True)  48.5 us
    all_to_all x1, waiting for transfers between devices, per_device(): lax.all_to_all(spread(final_mapping_matrix), 'sample', split_axis=1, conc...  38.5 us
    reduce_scatter x1, waiting for transfers between devices, per_device(): lax.psum_scatter(lax.dot_general(out_mine, answer_rows, (((1,), (1,)), ((...  37.8 us
  transfers between devices with their start and end apart: 8, of which 7 were waited for; matrix products, arithmetic and copies ran while one was open for 7% of the time, Pallas kernels for 0%

commit v1 on v0

v1 whole, which is shorter than its diff:
```python
import functools

import jax
import jax.numpy as jnp
from jax import lax
from jax.experimental import pallas as pl
from jax.experimental.pallas import tpu as pltpu
from jax.sharding import PartitionSpec as P

NORM_EPS = 1e-05
SLOTS = 8
VMEM = pl.BlockSpec(memory_space=pltpu.VMEM)
SMEM = pl.BlockSpec(memory_space=pltpu.SMEM)
ANY = pl.BlockSpec(memory_space=pl.ANY)
F32 = jnp.float32
BF16 = jnp.bfloat16


def normalize_kernel(x_ref, gain_ref, out_ref, rows):
    steps, held, width = x_ref.shape
    blocks, _, block = out_ref.shape
    gain = gain_ref[...].astype(F32)
    for i in range(steps):
        x = x_ref[i].astype(F32)
        scale = lax.rsqrt(jnp.mean(x * x, -1, keepdims=True) + NORM_EPS)
        rows[held * i : held * (i + 1), :] = x * scale * gain
    for b in range(blocks):
        out_ref[b] = rows[:, block * b : block * (b + 1)].astype(BF16)


def project_kernel(place_ref, x_ref, q_ref, kv_ref, out_ref):
    padded, rows = out_ref.shape[0], x_ref.shape[0]
    spread = (
        lax.broadcasted_iota(jnp.int32, (padded, rows), 0) == place_ref[...]
    ).astype(BF16)
    x = jnp.dot(spread, x_ref[...], preferred_element_type=F32).astype(BF16)
    width = q_ref.shape[1]
    for c in range(0, width, 256):
        out_ref[:, c : c + 256] = jnp.dot(
            x, q_ref[:, c : c + 256], preferred_element_type=F32
        ).astype(BF16)
    out_ref[:, width:] = jnp.dot(x, kv_ref[...], preferred_element_type=F32).astype(BF16)


def attend_kernel(heads, steps, ids_ref, extents_ref, part_ref, cache_ref, out_ref, cache, summed, answer, picked, sems):
    me = lax.axis_index("sample")
    owned = cache_ref.shape[0]
    head = cache_ref.shape[-1]
    extent = cache_ref.shape[-2]
    rows = steps * SLOTS
    for k in range(SLOTS):
        picked[k] = 0

    def look(j, found):
        row = ids_ref[j]
        mine = row // owned == me

        @pl.when(mine)
        def _():
            picked[found] = row % owned

        return found + mine.astype(jnp.int32)

    lax.fori_loop(0, ids_ref.shape[0], look, 0)
    copies = [
        pltpu.make_async_copy(cache_ref.at[picked[k]], cache.at[k], sems.at[k]) for k in range(SLOTS)
    ]
    for copy in copies:
        copy.start()
    for c in range(heads + 2):
        total = part_ref[0, :, head * c : head * (c + 1)].astype(F32)
        for source in range(1, part_ref.shape[0]):
            total = total + part_ref[source, :, head * c : head * (c + 1)].astype(F32)
        summed[rows * c : rows * (c + 1), :] = total
    many = heads * steps
    step_of = lax.broadcasted_iota(jnp.int32, (many, 16), 0) % steps
    fresh_at = lax.broadcasted_iota(jnp.int32, (many, 16), 1)
    causal = fresh_at <= step_of
    position = lax.broadcasted_iota(jnp.int32, (many, extent), 1)
    scale = head**-0.5
    nothing = jnp.zeros((16 - steps, head), F32)
    last = (((1,), (1,)), ((), ()))
    for k in range(SLOTS):
        query = summed[pl.ds(k, many, stride=SLOTS), :].astype(BF16)
        fresh_key = jnp.concatenate(
            [summed[pl.ds(rows * heads + k, steps, stride=SLOTS), :], nothing], 0
        ).astype(BF16)
        fresh_value = jnp.concatenate(
            [summed[pl.ds(rows * (heads + 1) + k, steps, stride=SLOTS), :], nothing], 0
        ).astype(BF16)
        length = extents_ref[me * owned + picked[k]]
        copies[k].wait()
        score = lax.dot_general(query, cache[k, 0], last, preferred_element_type=F32) * scale
        score = jnp.where(position < length, score, -jnp.inf)
        fresh = lax.dot_general(query, fresh_key, last, preferred_element_type=F32) * scale
        fresh = jnp.where(causal, fresh, -jnp.inf)
        highest = jnp.maximum(
            jnp.max(score, -1, keepdims=True), jnp.max(fresh, -1, keepdims=True)
        )
        probs = jnp.exp(score - highest)
        fresh_probs = jnp.exp(fresh - highest)
        total = jnp.sum(probs, -1, keepdims=True) + jnp.sum(fresh_probs, -1, keepdims=True)
        value = jnp.dot(probs.astype(BF16), cache[k, 1], preferred_element_type=F32)
        value = value + jnp.dot(fresh_probs.astype(BF16), fresh_value, preferred_element_type=F32)
        answer[pl.ds(k, many, stride=SLOTS), :] = value / total
    for h in range(heads):
        out_ref[:, head * h : head * (h + 1)] = answer[rows * h : rows * (h + 1), :].astype(BF16)


def output_kernel(place_ref, att_ref, w_ref, out_ref):
    rows, padded = out_ref.shape[0], att_ref.shape[0]
    pick = (lax.broadcasted_iota(jnp.int32, (rows, padded), 1) == place_ref[...]).astype(BF16)
    att = jnp.dot(pick, att_ref[...], preferred_element_type=F32).astype(BF16)
    for c in range(0, out_ref.shape[1], 256):
        out_ref[:, c : c + 256] = lax.dot_general(
            att, w_ref[c : c + 256, :], (((1,), (1,)), ((), ())), preferred_element_type=F32
        ).astype(BF16)


def coordinates(device):
    s, t = divmod(device, 8)
    return s >> 3, (s >> 1) & 3, s & 1, t >> 2, t & 3


def index_of(z_hi, x, core, z_lo, y):
    return ((z_hi * 4 + x) * 2 + core) * 8 + z_lo * 4 + y


def send(value, where):
    return lax.ppermute(
        value, ("sample", "tensor"), [(d, index_of(*where(*coordinates(d)))) for d in range(128)]
    )


def per_device(x, gain, probe, paired, final, memory, ids, extents):
    blocks = lax.axis_size("sample")
    parts = lax.axis_size("tensor")
    steps, held, width = x.shape
    block = width // blocks
    survivors = ids.shape[0]
    owned, _, _, extent, head = memory.shape
    q_width = probe.shape[2]
    heads = q_width // head
    kv_width = paired.shape[2]
    rows = steps * survivors
    slot_rows = steps * SLOTS
    padded = blocks * slot_rows

    owner = ids // owned
    at = jnp.arange(survivors)
    slot = jnp.sum((owner[:, None] == owner[None, :]) & (at[None, :] < at[:, None]), 1)
    place = (owner * slot_rows + slot).astype(jnp.int32)
    step_at = jnp.arange(steps, dtype=jnp.int32) * SLOTS
    place_in = (place.reshape(blocks, 1, held) + step_at[None, :, None]).reshape(1, rows)
    place_out = (place.reshape(blocks, 1, held) + step_at[None, :, None]).reshape(rows, 1)

    normed = pl.pallas_call(
        normalize_kernel,
        out_shape=jax.ShapeDtypeStruct((blocks, steps * held, block), BF16),
        in_specs=[VMEM, VMEM],
        out_specs=VMEM,
        scratch_shapes=[pltpu.VMEM((steps * held, width), F32)],
        name="normalize",
    )(x, gain.reshape(1, width))
    arrived = lax.all_to_all(normed, "sample", split_axis=0, concat_axis=0, tiled=True)

    partial = pl.pallas_call(
        project_kernel,
        out_shape=jax.ShapeDtypeStruct((padded, q_width + kv_width), BF16),
        in_specs=[VMEM] * 4,
        out_specs=VMEM,
        name="project",
        compiler_params=pltpu.CompilerParams(vmem_limit_bytes=24 << 20),
    )(place_in, arrived.reshape(rows, block), probe.reshape(block, q_width), paired.reshape(block, kv_width))
    mine = lax.all_to_all(
        partial.reshape(blocks, slot_rows, q_width + kv_width), "sample", split_axis=0, concat_axis=0, tiled=True
    )

    attended = pl.pallas_call(
        functools.partial(attend_kernel, heads, steps),
        out_shape=jax.ShapeDtypeStruct((slot_rows, q_width), BF16),
        in_specs=[SMEM, SMEM, VMEM, ANY],
        out_specs=VMEM,
        scratch_shapes=[
            pltpu.VMEM((SLOTS, 2, extent, head), BF16),
            pltpu.VMEM((slot_rows * (heads + 2), head), F32),
            pltpu.VMEM((slot_rows * heads, head), F32),
            pltpu.SMEM((SLOTS,), jnp.int32),
            pltpu.SemaphoreType.DMA((SLOTS,)),
        ],
        name="attend",
        compiler_params=pltpu.CompilerParams(vmem_limit_bytes=24 << 20),
    )(ids, extents, mine, memory.reshape(owned, 2, extent, head))
    gathered = lax.all_to_all(
        jnp.broadcast_to(attended[None], (blocks,) + attended.shape), "sample", split_axis=0, concat_axis=0, tiled=True
    )

    out = pl.pallas_call(
        output_kernel,
        out_shape=jax.ShapeDtypeStruct((rows, block), BF16),
        in_specs=[VMEM] * 3,
        out_specs=VMEM,
        name="output",
        compiler_params=pltpu.CompilerParams(vmem_limit_bytes=24 << 20),
    )(place_out, gathered.reshape(padded, q_width), final.reshape(block, q_width))
    out = lax.all_to_all(
        out.reshape(parts, rows // parts, block), "tensor", split_axis=0, concat_axis=0, tiled=True
    )
    out = jnp.sum(out.astype(F32), 0).astype(BF16).reshape(2, steps * held, block)
    core = lax.axis_index("sample") % 2
    kept = lax.dynamic_index_in_dim(out, core, 0, keepdims=False)
    other = send(
        lax.dynamic_index_in_dim(out, 1 - core, 0, keepdims=False),
        lambda z_hi, x, core, z_lo, y: (z_hi, x, 1 - core, z_lo, y),
    )
    both = jnp.where(core == 0, jnp.concatenate([kept, other], 1), jnp.concatenate([other, kept], 1))
    return send(both, lambda z_hi, x, core, z_lo, y: (z_lo, y, core, z_hi, x)).reshape(
        steps, held, width // parts
    )


def solution(mesh):
    placed = (
        P(None, "sample", None),
        P(),
        P("sample", "tensor", None),
        P("sample", "tensor", None),
        P("sample", "tensor", None),
        P("sample", "tensor", None, None, None),
        P(),
        P(),
    )
    return jax.shard_map(
        per_device,
        mesh=mesh,
        in_specs=placed,
        out_specs=P(None, "sample", "tensor"),
        check_vma=False,
    )
```

time: 393 us -> 97.5 us (0.25)
  waiting for transfers between devices: 249 us -> 37 us
  blocking collectives: 59.4 us -> 23.4 us
  local copies, waits for them, and re-layouts: 26 us -> 4.45 us
  between operations: 13.7 us -> 0.11 us
  matrix products: 12.5 us -> 0 us
  Pallas kernels: 0 us -> 9.46 us
  other arithmetic: 7.59 us -> 1.64 us
    ppermute x4 -> x2, waiting for transfers between devices: 124 us -> 6.42 us  [send(): lax.ppermute(value, ('sample', 'tensor'), [(d, index_of(*where(*coordinat...]
    all_to_all x3, waiting for transfers between devices: 87 us -> 30.6 us  [the longest x1 17.8 us: per_device(): lax.all_to_all(jnp.broadcast_to(attended[None], (blocks,) + attended.shap...]
    reduce_scatter x1 -> x0, waiting for transfers between devices: 37.8 us -> none  [per_device(): lax.psum_scatter(lax.dot_general(out_mine, answer_rows, (((1,), (1,)), ((...]
    all_to_all x1, blocking collectives: 59.4 us -> 23.4 us  [per_device(): lax.all_to_all(partial.reshape(blocks, slot_rows, q_width + kv_width), 's...]
    dot_general x7 -> x0, matrix products: 12.5 us -> none  [the longest x1 4.54 us: per_device(): lax.dot_general(out_mine, answer_rows, (((1,), (1,)), ((), ())), preferre...]
    gather x3 -> x0, local copies, waits for them, and re-layouts: 11.5 us -> none  [the longest x1 6.4 us: per_device(): jnp.take(arrived.reshape(blocks * CAP, 2, cache_len, head_size), pick_row...]
    pallas_call x0 -> x4, Pallas kernels: none -> 9.46 us  [the longest x1 4.97 us: per_device(): pl.pallas_call(functools.partial(attend_kernel, heads, steps), out_shape=...]
    broadcast_in_dim x2 -> x1, local copies, waits for them, and re-layouts: 7.58 us -> 1.09 us  [per_device(): jnp.broadcast_to(attended[None], (blocks,) + attended.shape)]
  transfers between devices with their start and end apart: 8 -> 5, of which waited for: 7 -> 5; matrix products, arithmetic and copies ran while one was open for 7% -> 2% of each run, Pallas kernels for 0% -> 0%
where the time goes in v1:
time: 97.5 us; the launch traced here: 97 us
  waiting for transfers between devices  37 us (38%)
  blocking collectives  23.4 us (24%)
  starting transfers between devices  20.9 us (21%)
  Pallas kernels  9.46 us (10%)
  local copies, waits for them, and re-layouts  4.45 us (5%)
  other arithmetic  1.64 us (2%)
    all_to_all x1, blocking collectives, per_device(): lax.all_to_all(partial.reshape(blocks, slot_rows, q_width + kv_width), 's...  23.4 us
    all_to_all x1, waiting for transfers between devices, per_device(): lax.all_to_all(jnp.broadcast_to(attended[None], (blocks,) + attended.shap...  17.8 us
    all_to_all x1, starting transfers between devices, per_device(): lax.all_to_all(normed, 'sample', split_axis=0, concat_axis=0, tiled=True)  7.72 us
    all_to_all x1, waiting for transfers between devices, per_device(): lax.all_to_all(normed, 'sample', split_axis=0, concat_axis=0, tiled=True)  7.58 us
    ppermute x2, waiting for transfers between devices, send(): lax.ppermute(value, ('sample', 'tensor'), [(d, index_of(*where(*coordinat...  6.42 us
    all_to_all x1, waiting for transfers between devices, per_device(): lax.all_to_all(out.reshape(parts, rows // parts, block), 'tensor', split_...  5.16 us
    all_to_all x1, starting transfers between devices, per_device(): lax.all_to_all(out.reshape(parts, rows // parts, block), 'tensor', split_...  5.15 us
    pallas_call x1, Pallas kernels, per_device(): pl.pallas_call(functools.partial(attend_kernel, heads, steps), out_shape=...  4.97 us
  transfers between devices with their start and end apart: 5, of which 5 were waited for; matrix products, arithmetic and copies ran while one was open for 2% of the time, Pallas kernels for 0%

profile of v1, /device:TPU:24, one launch (start us, length us, event | category | flops | bytes accessed | tf_op | source)
XLA Modules:
  0.0 97.0 jit_solution(3419522754232954638)
XLA Ops:
  0.0 0.0 copy-start.1
  0.0 1.4 %reshape.89.gain_ref = bf16[1,8192]{1,0:T(2,128)(2,1)} reshape(bf16[8192]{0:T(1024)(128)(2,1)} %param.9) | data formatting | bytes 32768 | tf_op jit(solution)/shard_map/reshape | solution.py:164
  1.4 2.0 %normalize.1 = bf16[16,16,512]{2,1,0:T(8,128)(2,1)} custom-call(bf16[4,4,8192]{2,1,0:T(4,128)(2,1)} %x_ref.1, bf16[1,8192]{1,0:T(2,128)(2,1)} %reshape.89.gain_ref), custom_call_target="tpu_custom_call" | custom-call | tf_op jit(solution)/shard_map/normalize/pallas_call | solution.py:157
  3.4 7.7 %all-to-all-start = ((bf16[16,16,512]{2,1,0:T(8,128)(2,1)}), bf16[16,16,512]{2,1,0:T(8,128)(2,1)S(1)}, u32[]{:S(2)}, u32[]{:S(2)}) async-start(bf16[16,16,512]{2,1,0:T(8,128)(2,1)} %normalize.1), calls=%async_computation | async-start | bytes 524288 | tf_op jit(solution)/shard_map/all_to_all | solution.py:165
  11.1 0.7 and_select_fusion
  11.8 0.2 convert_reduce_fusion
  12.0 0.7 multiply_add_fusion
  12.6 0.1 add.60
  12.7 0.1 broadcast_add_fusion
  12.8 0.1 add.65.place_ref
  12.9 7.6 %all-to-all-done = bf16[16,16,512]{2,1,0:T(8,128)(2,1)S(1)} async-done(((bf16[16,16,512]{2,1,0:T(8,128)(2,1)}), bf16[16,16,512]{2,1,0:T(8,128)(2,1)S(1)}, u32[]{:S(2)}, u32[]{:S(2)}) %all-to-all-start) | async-done | bytes 262176 | tf_op jit(solution)/shard_map/all_to_all | solution.py:165
  20.5 0.0 copy-done.1
  20.5 0.0 copy-start.3
  20.5 0.9 copy-done.3
  21.5 0.0 copy-start
  21.5 1.1 %project.1 = bf16[512,1280]{1,0:T(8,128)(2,1)S(1)} custom-call(s32[1,256]{1,0:T(1,128)S(1)} %add.65.place_ref, bf16[256,512]{1,0:T(8,128)(2,1)S(1)} %bitcast.18, bf16[512,1024]{1,0:T(8,128)(2,1)S(1)} %bitcast.16, bf16[512,256]{1,0:T(8,128)(2,1)S(1)} %bitcast.19), custom_call_target="tpu_custom_call" | custom-call | tf_op jit(solution)/shard_map/project/pallas_call | solution.py:167
  22.5 0.0 copy-start.4
  22.6 0.0 copy-start.5
  22.6 23.4 %all_to_all.20.part_ref = bf16[16,32,1280]{2,1,0:T(8,128)(2,1)S(1)} all-to-all(bf16[16,32,1280]{2,1,0:T(8,128)(2,1)S(1)} %bitcast.13), channel_id=1, replica_groups=mesh['sample'=16,'tensor'=8] {'sample'}, dimensions={0} | all-to-all | bytes 2621440 | tf_op jit(solution)/shard_map/all_to_all | solution.py:175
  45.9 0.0 copy-done
  45.9 0.0 copy-done.4
  45.9 0.0 copy-done.5
  45.9 5.0 %attend.1 = bf16[32,1024]{1,0:T(8,128)(2,1)S(1)} custom-call(s32[64]{0:T(128)S(1)} %copy-done.5, s32[256]{0:T(256)S(1)} %copy-done.4, bf16[16,32,1280]{2,1,0:T(8,128)(2,1)S(1)} %all_to_all.20.part_ref, bf16[16,2,512,128]{3,2,1,0:T(8,128)(2,1)S(1)} %bitcast.14), custom_call_target="tpu_custom_call" | custom-call | tf_op jit(solution)/shard_map/attend/pallas_call | solution.py:179
  50.9 1.1 %broadcast_in_dim.2 = bf16[16,32,1024]{2,1,0:T(8,128)(2,1)} broadcast(bf16[32,1024]{1,0:T(8,128)(2,1)S(1)} %attend.1), dimensions={1,2} | broadcast | bytes 1114112 | tf_op jit(solution)/shard_map/broadcast_in_dim | solution.py:195
  52.0 0.0 copy-start.2
  52.0 3.8 %all-to-all-start.2 = ((bf16[16,32,1024]{2,1,0:T(8,128)(2,1)}), bf16[16,32,1024]{2,1,0:T(8,128)(2,1)S(1)}, u32[]{:S(2)}, u32[]{:S(2)}) async-start(bf16[16,32,1024]{2,1,0:T(8,128)(2,1)} %broadcast_in_dim.2), calls=%async_computation.2 | async-start | bytes 2097152 | tf_op jit(solution)/shard_map/all_to_all | solution.py:194
  55.8 0.1 add.68.place_ref
  55.9 17.8 %all-to-all-done.2 = bf16[16,32,1024]{2,1,0:T(8,128)(2,1)S(1)} async-done(((bf16[16,32,1024]{2,1,0:T(8,128)(2,1)}), bf16[16,32,1024]{2,1,0:T(8,128)(2,1)S(1)}, u32[]{:S(2)}, u32[]{:S(2)}) %all-to-all-start.2) | async-done | bytes 1048608 | tf_op jit(solution)/shard_map/all_to_all | solution.py:194
  73.7 0.0 copy-done.2
  73.8 1.4 %output.1 = bf16[256,512]{1,0:T(8,128)(2,1)} custom-call(s32[256,1]{1,0:T(8,128)S(1)} %add.68.place_ref, bf16[512,1024]{1,0:T(8,128)(2,1)S(1)} %bitcast.15, bf16[512,1024]{1,0:T(8,128)(2,1)S(1)} %bitcast.17), custom_call_target="tpu_custom_call" | custom-call | tf_op jit(solution)/shard_map/output/pallas_call | solution.py:198
  75.2 5.1 %all-to-all-start.3 = ((bf16[8,32,512]{2,1,0:T(8,128)(2,1)}), bf16[8,32,512]{2,1,0:T(8,128)(2,1)S(1)}, u32[]{:S(2)}, u32[]{:S(2)}) async-start(bf16[8,32,512]{2,1,0:T(8,128)(2,1)} %bitcast.7), calls=%async_computation.3 | async-start | bytes 524288 | tf_op jit(solution)/shard_map/all_to_all | solution.py:206
  80.3 5.2 %all-to-all-done.3 = bf16[8,32,512]{2,1,0:T(8,128)(2,1)S(1)} async-done(((bf16[8,32,512]{2,1,0:T(8,128)(2,1)}), bf16[8,32,512]{2,1,0:T(8,128)(2,1)S(1)}, u32[]{:S(2)}, u32[]{:S(2)}) %all-to-all-start.3) | async-done | bytes 262176 | tf_op jit(solution)/shard_map/all_to_all | solution.py:206
  85.6 0.1 collective-permute-start
  85.7 1.2 %collective-permute-done = bf16[16,512]{1,0:T(8,128)(2,1)S(1)} collective-permute-done((bf16[16,512]{1,0:T(8,128)(2,1)S(1)}, bf16[16,512]{1,0:T(8,128)(2,1)S(1)}, u32[]{:S(2)}, u32[]{:S(2)}) %collective-permute-start) | collective-permute-done | bytes 16416 | tf_op jit(solution)/shard_map/ppermute | solution.py:130
  86.8 4.2 %collective-permute-start.1 = (bf16[16,1024]{1,0:T(8,128)(2,1)S(1)}, bf16[16,1024]{1,0:T(8,128)(2,1)S(1)}, u32[]{:S(2)}, u32[]{:S(2)}) collective-permute-start(bf16[16,1024]{1,0:T(8,128)(2,1)S(1)} %maximum_select_fusion), channel_id=1, source_target_pairs={{0,0},{1,16},{2,32},{3,48},{4,64},{5,80},{6,96},{7,112},{8,8},{9,2... | collective-permute-start | bytes 98312 | tf_op jit(solution)/shard_map/ppermute | solution.py:130
  91.1 5.3 %collective-permute-done.1 = bf16[16,1024]{1,0:T(8,128)(2,1)S(1)} collective-permute-done((bf16[16,1024]{1,0:T(8,128)(2,1)S(1)}, bf16[16,1024]{1,0:T(8,128)(2,1)S(1)}, u32[]{:S(2)}, u32[]{:S(2)}) %collective-permute-start.1) | collective-permute-done | bytes 32800 | tf_op jit(solution)/shard_map/ppermute | solution.py:130
  96.3 0.6 reshape.99
  (4 shorter events, 0.1 us)
Async XLA Ops:
  0.0 20.5 %copy-start.1 = (bf16[512,1,1024]{2,0,1:T(8,128)(2,1)S(1)}, bf16[512,1,1024]{2,0,1:T(8,128)(2,1)}, u32[]{:S(2)}) copy-start(bf16[512,1,1024]{2,0,1:T(8,128)(2,1)} %param.10) | copy-start | bytes 3145732
  3.4 17.1 %all-to-all-start = ((bf16[16,16,512]{2,1,0:T(8,128)(2,1)}), bf16[16,16,512]{2,1,0:T(8,128)(2,1)S(1)}, u32[]{:S(2)}, u32[]{:S(2)}) async-start(bf16[16,16,512]{2,1,0:T(8,128)(2,1)} %normalize.1), calls=%async_computation | async-start | bytes 524288 | tf_op jit(solution)/shard_map/all_to_all | solution.py:165
  20.5 1.0 copy-start.3
  21.5 24.5 %copy-start = (bf16[16,1,2,512,128]{4,3,2,1,0:T(8,128)(2,1)S(1)}, bf16[16,1,2,512,128]{4,3,2,1,0:T(8,128)(2,1)}, u32[]{:S(2)}) copy-start(bf16[16,1,2,512,128]{4,3,2,1,0:T(8,128)(2,1)} %param.13) | copy-start | bytes 12582916
  22.5 23.4 %copy-start.4 = (s32[256]{0:T(256)S(1)}, s32[256]{0:T(256)}, u32[]{:S(2)}) copy-start(s32[256]{0:T(256)} %extents_ref.1) | copy-start | bytes 3076
  22.6 23.4 %copy-start.5 = (s32[64]{0:T(128)S(1)}, s32[64]{0:T(128)}, u32[]{:S(2)}) copy-start(s32[64]{0:T(128)} %ids_ref.1) | copy-start | bytes 772
  52.0 21.7 %copy-start.2 = (bf16[512,1,1024]{2,0,1:T(8,128)(2,1)S(1)}, bf16[512,1,1024]{2,0,1:T(8,128)(2,1)}, u32[]{:S(2)}) copy-start(bf16[512,1,1024]{2,0,1:T(8,128)(2,1)} %param.12) | copy-start | bytes 3145732
  52.0 21.7 %all-to-all-start.2 = ((bf16[16,32,1024]{2,1,0:T(8,128)(2,1)}), bf16[16,32,1024]{2,1,0:T(8,128)(2,1)S(1)}, u32[]{:S(2)}, u32[]{:S(2)}) async-start(bf16[16,32,1024]{2,1,0:T(8,128)(2,1)} %broadcast_in_dim.2), calls=%async_computation.2 | async-start | bytes 2097152 | tf_op jit(solution)/shard_map/all_to_all | solution.py:194
  75.2 10.3 %all-to-all-start.3 = ((bf16[8,32,512]{2,1,0:T(8,128)(2,1)}), bf16[8,32,512]{2,1,0:T(8,128)(2,1)S(1)}, u32[]{:S(2)}, u32[]{:S(2)}) async-start(bf16[8,32,512]{2,1,0:T(8,128)(2,1)} %bitcast.7), calls=%async_computation.3 | async-start | bytes 524288 | tf_op jit(solution)/shard_map/all_to_all | solution.py:206
  85.6 1.3 %collective-permute-start = (bf16[16,512]{1,0:T(8,128)(2,1)S(1)}, bf16[16,512]{1,0:T(8,128)(2,1)S(1)}, u32[]{:S(2)}, u32[]{:S(2)}) collective-permute-start(bf16[16,512]{1,0:T(8,128)(2,1)S(1)} %get-tuple-element.6), channel_id=1, source_target_pairs={{0,8},{1,9},{2,10},{3,11},{4,12},{5,13},{6,14},{7,15},{8,0},{9,1},... | collective-permute-start | bytes 49160 | tf_op jit(solution)/shard_map/ppermute | solution.py:130
  86.8 9.5 %collective-permute-start.1 = (bf16[16,1024]{1,0:T(8,128)(2,1)S(1)}, bf16[16,1024]{1,0:T(8,128)(2,1)S(1)}, u32[]{:S(2)}, u32[]{:S(2)}) collective-permute-start(bf16[16,1024]{1,0:T(8,128)(2,1)S(1)} %maximum_select_fusion), channel_id=1, source_target_pairs={{0,0},{1,16},{2,32},{3,48},{4,64},{5,80},{6,96},{7,112},{8,8},{9,2... | collective-permute-start | bytes 98312 | tf_op jit(solution)/shard_map/ppermute | solution.py:130

commit v2 on v1

v2 whole, which is shorter than its diff:
```python
import functools

import jax
import jax.numpy as jnp
import numpy as np
from jax import lax
from jax.experimental import pallas as pl
from jax.experimental.pallas import tpu as pltpu
from jax.sharding import PartitionSpec as P

NORM_EPS = 1e-05
ROWS_ORDER = np.array([4, 5, 3, 7, 0, 1, 2, 6])
QUERY_ORDER = np.array([7, 6, 5, 4, 3, 2, 1, 0])
ATTENDED_ORDER = np.array([4, 5, 6, 2, 0, 1, 7, 3])
OUT_ORDER = np.array([2, 6, 5, 4, 3, 7, 1, 0])
SLOTS = 8
VMEM = pl.BlockSpec(memory_space=pltpu.VMEM)
SMEM = pl.BlockSpec(memory_space=pltpu.SMEM)
ANY = pl.BlockSpec(memory_space=pl.ANY)
F32 = jnp.float32
BF16 = jnp.bfloat16
I32 = jnp.int32
LAST = (((1,), (1,)), ((), ()))
FIRST = (((0,), (0,)), ((), ()))


def place_of(s, t):
    return s >> 3, (s >> 1) & 3, s & 1, t >> 2, t & 3


def send(value, where):
    pairs = []
    for device in range(128):
        z_hi, x, core, z_lo, y = where(*place_of(*divmod(device, 8)))
        pairs.append((device, ((z_hi * 4 + x) * 2 + core) * 8 + z_lo * 4 + y))
    return lax.ppermute(value, ("sample", "tensor"), pairs)


def to_core(z_hi, x, core, z_lo, y):
    return z_hi, x, 1 - core, z_lo, y


def summed_at(x, y):
    return (2 * x + 2 - y) & 3


def to_rows(z_hi, x, core, z_lo, y):
    return z_lo, summed_at(x, y), core, z_hi, x


def exchange_chips(value, order):
    return lax.all_to_all(
        value,
        "sample",
        split_axis=0,
        concat_axis=0,
        tiled=True,
        axis_index_groups=[[2 * chip + core for chip in order.tolist()] for core in range(2)],
    )


def exchange_rows(value):
    groups = [
        [(chip * 2 + core) * 8 + (z_lo ^ (chip >> 2)) * 4 + y for chip in ROWS_ORDER.tolist()]
        for core in range(2)
        for z_lo in range(2)
        for y in range(4)
    ]
    return lax.all_to_all(
        value, ("sample", "tensor"), split_axis=0, concat_axis=0, tiled=True, axis_index_groups=groups
    )


def exchange_heads(value):
    return lax.all_to_all(
        value, "tensor", split_axis=0, concat_axis=0, tiled=True, axis_index_groups=[OUT_ORDER.tolist()]
    )


def entry(order, at):
    found = 0
    for n, value in enumerate(order.tolist()):
        found = jnp.where(at == n, value, found)
    return found


def normalize_kernel(x_ref, gain_ref, out_ref, x_here, gain_here, rows, sems):
    steps, held, width = x_ref.shape
    chips, _, block = out_ref.shape
    gain_copy = pltpu.make_async_copy(gain_ref, gain_here, sems.at[0])
    x_copy = pltpu.make_async_copy(x_ref, x_here, sems.at[1])
    gain_copy.start()
    x_copy.start()
    gain_copy.wait()
    gain = gain_here[...].astype(F32).reshape(1, width)
    x_copy.wait()
    for i in range(steps):
        x = x_here[i].astype(F32)
        scale = lax.rsqrt(jnp.mean(x * x, -1, keepdims=True) + NORM_EPS)
        rows[held * i : held * (i + 1), :] = x * scale * gain
    for m in range(chips):
        at = block * int(ROWS_ORDER[m])
        out_ref[m] = rows[:, at : at + block].astype(BF16)


def project_kernel(key_ref, near_ref, far_ref, q_ref, kv_ref, out_ref, chosen):
    chips, rows, _ = out_ref.shape
    padded = chips * rows
    half = near_ref.shape[0]
    spread = (
        lax.broadcasted_iota(I32, (padded, 2 * half), 0) == key_ref[...]
    ).astype(BF16)
    x = jnp.dot(spread[:, :half], near_ref[...], preferred_element_type=F32)
    x = x + jnp.dot(spread[:, half:], far_ref[...], preferred_element_type=F32)
    chosen[...] = x.astype(BF16)
    core = lax.axis_index("sample") % 2
    block, width = q_ref.shape[0] // 2, q_ref.shape[1]
    mine = chosen[:, pl.ds(pl.multiple_of(core * block, block), block)]
    other = chosen[:, pl.ds(pl.multiple_of((1 - core) * block, block), block)]
    for c in range(0, width + kv_ref.shape[1], 256):
        w_ref, at = (q_ref, c) if c < width else (kv_ref, 0)
        w, w2 = w_ref[:block, at : at + 256], w_ref[block:, at : at + 256]
        part = jnp.dot(mine, w, preferred_element_type=F32)
        part = part + jnp.dot(other, w2, preferred_element_type=F32)
        part = part.astype(BF16)
        for m in range(chips):
            out_ref[m, :, c : c + 256] = part[rows * m : rows * (m + 1)]


def attend_kernel(heads, steps, picked_ref, length_ref, part_ref, cache_ref, out_ref, summed, answer):
    head = cache_ref.shape[-1]
    extent = cache_ref.shape[-2]
    rows = steps * SLOTS
    for c in range(heads + 2):
        total = part_ref[0, :, head * c : head * (c + 1)].astype(F32)
        for source in range(1, part_ref.shape[0]):
            total = total + part_ref[source, :, head * c : head * (c + 1)].astype(F32)
        summed[rows * c : rows * (c + 1), :] = total
    many = heads * steps
    scale = head**-0.5
    position = lax.broadcasted_iota(I32, (many, extent), 1)
    fresh_at = lax.broadcasted_iota(I32, (many, head), 1)
    causal = fresh_at <= lax.broadcasted_iota(I32, (many, head), 0) % steps
    nothing = jnp.zeros((head - steps, head), F32)

    def fresh(k, which):
        rows_at = pl.ds(rows * (heads + which) + k, steps, stride=SLOTS)
        return jnp.concatenate([summed[rows_at, :], nothing], 0).astype(BF16)

    scores = []
    for k in range(SLOTS):
        query = summed[pl.ds(k, many, stride=SLOTS), :].astype(BF16)
        scores.append(
            (
                lax.dot_general(query, cache_ref[picked_ref[k], 0], LAST, preferred_element_type=F32),
                lax.dot_general(query, fresh(k, 0), LAST, preferred_element_type=F32),
            )
        )
    weights = []
    for k in range(SLOTS):
        score = jnp.where(position < length_ref[k], scores[k][0] * scale, -jnp.inf)
        fresh_score = jnp.where(causal, scores[k][1] * scale, -jnp.inf)
        highest = fresh_score
        for c in range(0, extent, head):
            highest = jnp.maximum(highest, score[:, c : c + head])
        highest = jnp.max(highest, -1, keepdims=True)
        probs, fresh_probs = jnp.exp(score - highest), jnp.exp(fresh_score - highest)
        total = fresh_probs
        for c in range(0, extent, head):
            total = total + probs[:, c : c + head]
        total = jnp.sum(total, -1, keepdims=True)
        weights.append((probs.astype(BF16), fresh_probs.astype(BF16), total))
    for k in range(SLOTS):
        probs, fresh_probs, total = weights[k]
        value = jnp.dot(probs, cache_ref[picked_ref[k], 1], preferred_element_type=F32)
        value = value + jnp.dot(fresh_probs, fresh(k, 1), preferred_element_type=F32)
        answer[pl.ds(k, many, stride=SLOTS), :] = value / total
    for h in range(heads):
        part = answer[rows * h : rows * (h + 1), :].astype(BF16)
        for m in range(out_ref.shape[0]):
            out_ref[m, :, head * h : head * (h + 1)] = part


def output_kernel(key_ref, att_ref, w_ref, out_ref):
    rows = att_ref.shape[0]
    pick = (lax.broadcasted_iota(I32, (rows, out_ref.shape[0]), 0) == key_ref[...]).astype(BF16)
    att = lax.dot_general(pick, att_ref[...], FIRST, preferred_element_type=F32).astype(BF16)
    core = lax.axis_index("sample") % 2
    block = w_ref.shape[0] // 2
    for c in range(0, 2 * block, 256):
        out = lax.dot_general(
            att, w_ref[c : c + 256, :], LAST, preferred_element_type=F32
        ).astype(BF16)
        at = core * block if c < block else (1 - core) * block
        columns = pl.ds(pl.multiple_of(at + c % block, 256), 256)
        out_ref[:, columns] = out


def call(kernel, name, out_shape, specs, scratch=(), vmem=24, cost=None):
    return pl.pallas_call(
        kernel,
        out_shape=out_shape,
        in_specs=specs,
        out_specs=jax.tree.map(lambda _: VMEM, out_shape),
        scratch_shapes=list(scratch),
        name=name,
        cost_estimate=cost,
        compiler_params=pltpu.CompilerParams(vmem_limit_bytes=vmem << 20),
    )


def per_device(x, gain, probe, paired, final, memory, ids, extents):
    steps, held, width = x.shape
    survivors = ids.shape[0]
    owned, _, _, extent, head = memory.shape
    block, _, q_width = probe.shape
    heads = q_width // head
    kv_width = paired.shape[2]
    chips = lax.axis_size("sample") // 2
    chip_block = 2 * block
    rows = steps * survivors
    slot_rows = steps * SLOTS
    shape = jax.ShapeDtypeStruct

    probe, paired, final = (w.reshape(block, w.shape[2]) for w in (probe, paired, final))

    normed = call(
        normalize_kernel,
        "normalize",
        shape((chips, steps * held, chip_block), BF16),
        [ANY, ANY],
        [
            pltpu.VMEM((steps, held, width), BF16),
            pltpu.VMEM((width,), BF16),
            pltpu.VMEM((steps * held, width), F32),
            pltpu.SemaphoreType.DMA((2,)),
        ],
        vmem=60,
    )(x, gain)
    normed, final_out = lax.optimization_barrier((normed, final))
    probe2, paired2, final2 = (send(w, to_core) for w in (probe, paired, final_out))
    near = exchange_rows(normed)

    s = lax.axis_index("sample")
    core, x_at = s & 1, (s >> 1) & 3
    bits = owned.bit_length() - 1
    ids, probe2, paired2 = lax.optimization_barrier((ids, probe2, paired2))
    code = lax.optimization_barrier(ids ^ (s << bits))
    owner = (code >> bits) ^ s
    at = jnp.arange(survivors, dtype=I32)
    slot = jnp.sum(
        ((owner[:, None] == owner[None, :]) & (at[None, :] < at[:, None])).astype(I32), 1
    )
    key, key_back = (
        jnp.where(
            (owner & 1) == core,
            entry(np.argsort(order), owner >> 1) * slot_rows + slot,
            -(1 << 20),
        )
        for order in (QUERY_ORDER, ATTENDED_ORDER)
    )
    q = jnp.arange(rows, dtype=I32)
    n, held_at, step_at = q // (steps * held), q % held, q // held % steps * SLOTS
    this_core = core ^ (n // 8)
    source = (2 * entry(ROWS_ORDER, n % 8) + this_core) * held + held_at
    target_t = entry(OUT_ORDER, n % 8)
    target = (target_t // 4 * 8 + summed_at(x_at, target_t % 4) * 2 + this_core) * held + held_at
    key_in, key_out = (
        (jnp.sum(jnp.where(at[:, None] == j[None, :], keys[:, None], 0), 0) + step_at).reshape(1, rows)
        for j, keys in ((source, key), (target, key_back))
    )
    mine = (owner[:, None] == s) & (slot[:, None] == jnp.arange(SLOTS, dtype=I32)[None, :])
    picked = jnp.sum(jnp.where(mine, (code & (owned - 1))[:, None], 0), 0)
    row_at = s * owned + picked
    length = jnp.sum(
        jnp.where(row_at[:, None] == jnp.arange(extents.shape[0], dtype=I32)[None, :], extents[None, :], 0), 1
    )
    weights = jnp.concatenate([probe, probe2], 0)
    kv_weights = jnp.concatenate([paired, paired2], 0)
    near, key_in, key_out, picked, length, weights, kv_weights = lax.optimization_barrier(
        (near, key_in, key_out, picked, length, weights, kv_weights)
    )
    near = near.reshape(rows // 2, chip_block)
    far = send(near, to_core)

    partial = call(
        project_kernel,
        "project",
        shape((chips, slot_rows, q_width + kv_width), BF16),
        [VMEM] * 5,
        [pltpu.VMEM((rows, chip_block), BF16)],
    )(key_in, near, far, weights, kv_weights)
    attended = call(
        functools.partial(attend_kernel, heads, steps),
        "attend",
        shape((chips, slot_rows, q_width), BF16),
        [SMEM, SMEM, VMEM, VMEM],
        [
            pltpu.VMEM((slot_rows * (heads + 2), head), F32),
            pltpu.VMEM((slot_rows * heads, head), F32),
        ],
        vmem=48,
    )(picked, length, exchange_chips(partial, QUERY_ORDER), memory.reshape(owned, 2, extent, head))
    attended = exchange_chips(attended, ATTENDED_ORDER).reshape(rows, q_width)
    attended, final = lax.optimization_barrier((attended, jnp.concatenate([final, final2], 0)))
    sent, kept = (
        call(
            output_kernel,
            "output",
            shape((rows // 2, chip_block), BF16),
            [VMEM] * 3,
            cost=pl.CostEstimate(
                flops=rows * chip_block * q_width, bytes_accessed=4 << 20, transcendentals=0
            ),
        )(key_out[:, at : at + rows // 2], attended, final)
        for at in (rows // 2, 0)
    )
    out = kept + send(sent, to_core)
    out = exchange_heads(out.reshape(8, steps * held, chip_block))
    out = jnp.sum(out.astype(F32), 0).astype(BF16).reshape(steps, held, chip_block)
    return send(out, to_rows)


def solution(mesh):
    placed = (
        P(None, "sample", None),
        P(),
        P("sample", "tensor", None),
        P("sample", "tensor", None),
        P("sample", "tensor", None),
        P("sample", "tensor", None, None, None),
        P(),
        P(),
    )
    return jax.shard_map(
        per_device,
        mesh=mesh,
        in_specs=placed,
        out_specs=P(None, "sample", "tensor"),
        check_vma=False,
    )
```

time: 97.5 us -> 72.8 us (0.75)
  waiting for transfers between devices: 37 us -> 16.2 us
  starting transfers between devices: 20.9 us -> 17.1 us
  local copies, waits for them, and re-layouts: 4.45 us -> 0.66 us
  other arithmetic: 1.64 us -> 4.77 us
  blocking collectives: 23.4 us -> 25.6 us
  Pallas kernels: 9.46 us -> 7.53 us
    all_to_all x3 -> x2, waiting for transfers between devices: 30.6 us -> 8.71 us  [the longest x1 5.8 us: exchange_chips(): lax.all_to_all(value, 'sample', split_axis=0, concat_axis=0, tiled=True,...]
    concatenate x0 -> x3, other arithmetic: none -> 3.2 us  [the longest x1 1.71 us: per_device(): jnp.concatenate([final, final2], 0)]
    all_to_all x1 -> x2, blocking collectives: 23.4 us -> 25.6 us  [the longest x1 15.8 us: exchange_chips(): lax.all_to_all(value, 'sample', split_axis=0, concat_axis=0, tiled=True,...]
    reshape x2 -> x1, local copies, waits for them, and re-layouts: 2.07 us -> 0.02 us  [per_device(): jnp.sum(out.astype(F32), 0).astype(BF16).reshape(steps, held, chip_block)]
    all_to_all x3 -> x2, starting transfers between devices: 16.6 us -> 14.7 us  [the longest x1 8.35 us: exchange_rows(): lax.all_to_all(value, ('sample', 'tensor'), split_axis=0, concat_axis=0,...]
    pallas_call x4 -> x5, Pallas kernels: 9.46 us -> 7.53 us  [the longest x1 2.23 us: per_device(): call(functools.partial(attend_kernel, heads, steps), 'attend', shape((chi...]
    ppermute x2 -> x6, starting transfers between devices: 4.3 us -> 2.49 us  [send(): return lax.ppermute(value, ('sample', 'tensor'), pairs)]
    ppermute x2 -> x6, waiting for transfers between devices: 6.42 us -> 7.52 us  [send(): return lax.ppermute(value, ('sample', 'tensor'), pairs)]
  transfers between devices with their start and end apart: 5 -> 8, of which waited for: 5 -> 5; matrix products, arithmetic and copies ran while one was open for 2% -> 6% of each run, Pallas kernels for 0% -> 9%
where the time goes in v2:
time: 72.8 us; the launch traced here: 72.1 us
  blocking collectives  25.6 us (35%)
  starting transfers between devices  17.1 us (23%)
  waiting for transfers between devices  16.2 us (22%)
  Pallas kernels  7.53 us (10%)
  other arithmetic  4.77 us (7%)
    all_to_all x1, blocking collectives, exchange_chips(): lax.all_to_all(value, 'sample', split_axis=0, concat_axis=0, tiled=True,...  15.8 us
    all_to_all x1, blocking collectives, exchange_heads(): lax.all_to_all(value, 'tensor', split_axis=0, concat_axis=0, tiled=True,...  9.83 us
    all_to_all x1, starting transfers between devices, exchange_rows(): lax.all_to_all(value, ('sample', 'tensor'), split_axis=0, concat_axis=0,...  8.35 us
    ppermute x6, waiting for transfers between devices, send(): return lax.ppermute(value, ('sample', 'tensor'), pairs)  7.52 us
    all_to_all x1, starting transfers between devices, exchange_chips(): lax.all_to_all(value, 'sample', split_axis=0, concat_axis=0, tiled=True,...  6.31 us
    all_to_all x1, waiting for transfers between devices, exchange_chips(): lax.all_to_all(value, 'sample', split_axis=0, concat_axis=0, tiled=True,...  5.8 us
    all_to_all x1, waiting for transfers between devices, exchange_rows(): lax.all_to_all(value, ('sample', 'tensor'), split_axis=0, concat_axis=0,...  2.91 us
    ppermute x6, starting transfers between devices, send(): return lax.ppermute(value, ('sample', 'tensor'), pairs)  2.49 us
  transfers between devices with their start and end apart: 8, of which 5 were waited for; matrix products, arithmetic and copies ran while one was open for 6% of the time, Pallas kernels for 9%

profile of v2, /device:TPU:24, one launch (start us, length us, event | category | flops | bytes accessed | tf_op | source)
XLA Modules:
  0.0 72.1 jit_solution(4743165906120548451)
XLA Ops:
  0.0 0.0 collective-permute-start
  0.0 0.5 collective-permute-start.1
  0.5 2.0 %normalize.1 = bf16[8,16,1024]{2,1,0:T(8,128)(2,1)} custom-call(bf16[4,4,8192]{2,1,0:T(4,128)(2,1)} %x_ref.1, bf16[8192]{0:T(1024)(128)(2,1)} %gain_ref.1), custom_call_target="tpu_custom_call" | custom-call | tf_op jit(solution)/shard_map/normalize/pallas_call | solution.py:227
  2.5 8.3 %all-to-all-start = ((bf16[8,16,1024]{2,1,0:T(8,128)(2,1)}), bf16[8,16,1024]{2,1,0:T(8,128)(2,1)S(1)}, u32[]{:S(2)}, u32[]{:S(2)}) async-start(bf16[8,16,1024]{2,1,0:T(8,128)(2,1)} %normalize.1), calls=%async_computation | async-start | bytes 524288 | tf_op jit(solution)/shard_map/all_to_all | solution.py:69
  10.9 0.0 collective-permute-start.3
  10.9 0.0 collective-permute-done.1
  10.9 0.0 copy-start.2
  10.9 0.0 collective-permute-done
  10.9 0.7 broadcast_xor_fusion
  11.6 0.2 convert_reduce_fusion
  11.8 0.1 select_reduce_fusion
  11.9 0.1 select_reduce_fusion.1
  12.0 0.0 copy-done.2
  12.1 0.0 copy-start.4
  12.1 0.0 copy-start.1
  12.1 0.0 copy-start.3
  12.1 1.5 %pad_maximum_fusion.q_ref = bf16[1024,1024]{1,0:T(8,128)(2,1)S(1)} fusion(bf16[512,1024]{1,0:T(8,128)(2,1)S(1)} %collective-permute-done, bf16[512,1024]{1,0:T(8,128)(2,1)} %bitcast.16), kind=kLoop, calls=%fused_computation | loop fusion | flops 4194304 | bytes 4194304 | tf_op jit(solution)/shard_map/concatenate | solution.py:278
  13.6 0.1 select_reduce_fusion.3.picked_ref
  13.7 0.0 copy-done.4
  13.7 0.2 select_reduce_fusion.2.length_ref
  13.9 0.0 copy-done.1
  13.9 0.0 copy-done.3
  13.9 2.9 %all-to-all-done = bf16[8,16,1024]{2,1,0:T(8,128)(2,1)S(1)} async-done(((bf16[8,16,1024]{2,1,0:T(8,128)(2,1)}), bf16[8,16,1024]{2,1,0:T(8,128)(2,1)S(1)}, u32[]{:S(2)}, u32[]{:S(2)}) %all-to-all-start) | async-done | bytes 262176 | tf_op jit(solution)/shard_map/all_to_all | solution.py:69
  16.8 0.0 copy-start
  16.8 0.0 collective-permute-start.2
  16.8 1.5 %collective-permute-done.2.far_ref = bf16[128,1024]{1,0:T(8,128)(2,1)S(1)} collective-permute-done((bf16[128,1024]{1,0:T(8,128)(2,1)S(1)}, bf16[128,1024]{1,0:T(8,128)(2,1)S(1)}, u32[]{:S(2)}, u32[]{:S(2)}) %collective-permute-start.2) | collective-permute-done | bytes 262176 | tf_op jit(solution)/shard_map/ppermute | solution.py:36
  18.4 1.4 %project.1 = bf16[8,32,1280]{2,1,0:T(8,128)(2,1)S(1)} custom-call(s32[1,256]{1,0:T(1,128)S(1)} %fusion.14.key_ref, bf16[128,1024]{1,0:T(8,128)(2,1)S(1)} %bitcast.13, bf16[128,1024]{1,0:T(8,128)(2,1)S(1)} %collective-permute-done.2.far_ref, bf16[1024,1024]{1,0:T(8,128)(2,1)S(1)} %pad_maximum_fusion.q_ref, bf16[1024,256]{1,0:T(8,128)(2,1)S(1)} %pad_maximum_fusion.2.kv_ref), custom_call_target="tpu_custom_call" | custom-call | tf_op jit(solution)/shard_map/project/pallas_call | solution.py:286
  19.8 15.8 %all_to_all.20.part_ref = bf16[8,32,1280]{2,1,0:T(8,128)(2,1)S(1)} all-to-all(bf16[8,32,1280]{2,1,0:T(8,128)(2,1)S(1)} %project.1), channel_id=1, replica_groups={{112,96,80,64,48,32,16,0},{120,104,88,72,56,40,24,8},{113,97,81,65,49,3..., dimensions={0} | all-to-all | bytes 1310720 | tf_op jit(solution)/shard_map/all_to_all | solution.py:52
  35.6 0.0 copy-done
  35.6 2.2 %attend.1 = bf16[8,32,1024]{2,1,0:T(8,128)(2,1)} custom-call(s32[8]{0:T(128)S(1)} %select_reduce_fusion.3.picked_ref, s32[8]{0:T(128)S(1)} %select_reduce_fusion.2.length_ref, bf16[8,32,1280]{2,1,0:T(8,128)(2,1)S(1)} %all_to_all.20.part_ref, bf16[16,2,512,128]{3,2,1,0:T(8,128)(2,1)S(1)} %bitcast.11), custom_call_target="tpu_custom_call" | custom-call | tf_op jit(solution)/shard_map/attend/pallas_call | solution.py:293
  37.8 6.3 %all-to-all-start.2 = ((bf16[8,32,1024]{2,1,0:T(8,128)(2,1)}), bf16[8,32,1024]{2,1,0:T(8,128)(2,1)S(1)}, u32[]{:S(2)}, u32[]{:S(2)}) async-start(bf16[8,32,1024]{2,1,0:T(8,128)(2,1)} %attend.1), calls=%async_computation.2 | async-start | bytes 1048576 | tf_op jit(solution)/shard_map/all_to_all | solution.py:52
  44.1 0.0 collective-permute-done.3
  44.1 1.7 %pad_maximum_fusion.1.w_ref = bf16[1024,1024]{1,0:T(8,128)(2,1)S(1)} fusion(bf16[512,1024]{1,0:T(8,128)(2,1)} %collective-permute-done.3, bf16[512,1024]{1,0:T(8,128)(2,1)} %bitcast.18), kind=kLoop, calls=%fused_computation.1 | loop fusion | flops 4194304 | bytes 4194304 | tf_op jit(solution)/shard_map/concatenate | solution.py:305
  45.9 5.8 %all-to-all-done.2 = bf16[8,32,1024]{2,1,0:T(8,128)(2,1)S(1)} async-done(((bf16[8,32,1024]{2,1,0:T(8,128)(2,1)}), bf16[8,32,1024]{2,1,0:T(8,128)(2,1)S(1)}, u32[]{:S(2)}, u32[]{:S(2)}) %all-to-all-start.2) | async-done | bytes 524320 | tf_op jit(solution)/shard_map/all_to_all | solution.py:52
  51.7 0.9 %output.3 = bf16[128,1024]{1,0:T(8,128)(2,1)S(1)} custom-call(s32[1,128]{1,0:T(1,128)S(1)} %get-tuple-element.35.key_ref, bf16[256,1024]{1,0:T(8,128)(2,1)S(1)} %bitcast.9, bf16[1024,1024]{1,0:T(8,128)(2,1)S(1)} %pad_maximum_fusion.1.w_ref), custom_call_target="tpu_custom_call" | custom-call | flops 268435456 | bytes 4194304 | tf_op jit(solution)/shard_map/output/pallas_call | solution.py:307
  52.6 0.1 collective-permute-start.4
  52.7 0.9 %output.2 = bf16[128,1024]{1,0:T(8,128)(2,1)S(1)} custom-call(s32[1,128]{1,0:T(1,128)S(1)} %get-tuple-element.36.key_ref, bf16[256,1024]{1,0:T(8,128)(2,1)S(1)} %bitcast.10, bf16[1024,1024]{1,0:T(8,128)(2,1)S(1)} %pad_maximum_fusion.1.w_ref), custom_call_target="tpu_custom_call" | custom-call | flops 268435456 | bytes 4194304 | tf_op jit(solution)/shard_map/output/pallas_call | solution.py:307
  53.7 0.6 collective-permute-done.4
  54.2 0.1 add.185
  54.3 9.8 %all_to_all.21 = bf16[8,16,1024]{2,1,0:T(8,128)(2,1)S(1)} all-to-all(bf16[8,16,1024]{2,1,0:T(8,128)(2,1)S(1)} %bitcast.14), channel_id=1, replica_groups={{2,6,5,4,3,7,1,0},{10,14,13,12,11,15,9,8},{18,22,21,20,19,23,17,16},{26..., dimensions={0} | all-to-all | bytes 524288 | tf_op jit(solution)/shard_map/all_to_all | solution.py:75
  64.2 1.9 %collective-permute-start.5 = (bf16[4,4,1024]{2,1,0:T(4,128)(2,1)S(1)}, bf16[4,4,1024]{2,1,0:T(4,128)(2,1)S(1)}, u32[]{:S(2)}, u32[]{:S(2)}) collective-permute-start(bf16[4,4,1024]{2,1,0:T(4,128)(2,1)S(1)} %reshape.226), channel_id=1, source_target_pairs={{0,32},{1,16},{2,0},{3,48},{4,96},{5,80},{6,64},{7,112},{8,40},{9,... | collective-permute-start | bytes 98312 | tf_op jit(solution)/shard_map/ppermute | solution.py:36
  66.1 5.4 %collective-permute-done.5 = bf16[4,4,1024]{2,1,0:T(4,128)(2,1)S(1)} collective-permute-done((bf16[4,4,1024]{2,1,0:T(4,128)(2,1)S(1)}, bf16[4,4,1024]{2,1,0:T(4,128)(2,1)S(1)}, u32[]{:S(2)}, u32[]{:S(2)}) %collective-permute-start.5) | collective-permute-done | bytes 32800 | tf_op jit(solution)/shard_map/ppermute | solution.py:36
  71.5 0.6 copy.10
  (11 shorter events, 0.2 us)
Async XLA Ops:
  0.0 10.9 %collective-permute-start = (bf16[512,1024]{1,0:T(8,128)(2,1)}, bf16[512,1024]{1,0:T(8,128)(2,1)S(1)}, u32[]{:S(2)}, u32[]{:S(2)}) collective-permute-start(bf16[512,1024]{1,0:T(8,128)(2,1)} %bitcast.15), channel_id=1, source_target_pairs={{0,8},{1,9},{2,10},{3,11},{4,12},{5,13},{6,14},{7,15},{8,0},{9,1},... | collective-permute-start | bytes 3145736 | tf_op jit(solution)/shard_map/ppermute | solution.py:36
  0.0 10.9 %collective-permute-start.1 = (bf16[512,256]{1,0:T(8,128)(2,1)}, bf16[512,256]{1,0:T(8,128)(2,1)S(1)}, u32[]{:S(2)}, u32[]{:S(2)}) collective-permute-start(bf16[512,256]{1,0:T(8,128)(2,1)} %bitcast.19), channel_id=1, source_target_pairs={{0,8},{1,9},{2,10},{3,11},{4,12},{5,13},{6,14},{7,15},{8,0},{9,1},... | collective-permute-start | bytes 786440 | tf_op jit(solution)/shard_map/ppermute | solution.py:36
  2.5 14.3 %all-to-all-start = ((bf16[8,16,1024]{2,1,0:T(8,128)(2,1)}), bf16[8,16,1024]{2,1,0:T(8,128)(2,1)S(1)}, u32[]{:S(2)}, u32[]{:S(2)}) async-start(bf16[8,16,1024]{2,1,0:T(8,128)(2,1)} %normalize.1), calls=%async_computation | async-start | bytes 524288 | tf_op jit(solution)/shard_map/all_to_all | solution.py:69
  10.9 33.3 %collective-permute-start.3 = (bf16[512,1024]{1,0:T(8,128)(2,1)}, bf16[512,1024]{1,0:T(8,128)(2,1)}, u32[]{:S(2)}, u32[]{:S(2)}) collective-permute-start(bf16[512,1024]{1,0:T(8,128)(2,1)} %bitcast.17), channel_id=1, source_target_pairs={{0,8},{1,9},{2,10},{3,11},{4,12},{5,13},{6,14},{7,15},{8,0},{9,1},... | collective-permute-start | bytes 3145736 | tf_op jit(solution)/shard_map/ppermute | solution.py:36
  10.9 1.1 %copy-start.2 = (bf16[512,256]{1,0:T(8,128)(2,1)}, bf16[512,256]{1,0:T(8,128)(2,1)S(1)}, u32[]{:S(2)}) copy-start(bf16[512,256]{1,0:T(8,128)(2,1)S(1)} %collective-permute-done.1) | copy-start | bytes 786436
  12.1 1.6 %copy-start.4 = (s32[256]{0:T(256)S(1)}, s32[256]{0:T(256)}, u32[]{:S(2)}) copy-start(s32[256]{0:T(256)} %param.15) | copy-start | bytes 3076
  12.1 1.8 %copy-start.1 = (bf16[512,1,256]{2,0,1:T(8,128)(2,1)S(1)}, bf16[512,1,256]{2,0,1:T(8,128)(2,1)}, u32[]{:S(2)}) copy-start(bf16[512,1,256]{2,0,1:T(8,128)(2,1)} %param.11) | copy-start | bytes 786436
  12.1 1.8 %copy-start.3 = (bf16[512,256]{1,0:T(8,128)(2,1)S(1)}, bf16[512,256]{1,0:T(8,128)(2,1)}, u32[]{:S(2)}) copy-start(bf16[512,256]{1,0:T(8,128)(2,1)} %copy-done.2) | copy-start | bytes 786436
  16.8 18.8 %copy-start = (bf16[16,1,2,512,128]{4,3,2,1,0:T(8,128)(2,1)S(1)}, bf16[16,1,2,512,128]{4,3,2,1,0:T(8,128)(2,1)}, u32[]{:S(2)}) copy-start(bf16[16,1,2,512,128]{4,3,2,1,0:T(8,128)(2,1)} %param.13) | copy-start | bytes 12582916
  16.8 1.5 %collective-permute-start.2 = (bf16[128,1024]{1,0:T(8,128)(2,1)S(1)}, bf16[128,1024]{1,0:T(8,128)(2,1)S(1)}, u32[]{:S(2)}, u32[]{:S(2)}) collective-permute-start(bf16[128,1024]{1,0:T(8,128)(2,1)S(1)} %bitcast.12), channel_id=1, source_target_pairs={{0,8},{1,9},{2,10},{3,11},{4,12},{5,13},{6,14},{7,15},{8,0},{9,1},... | collective-permute-start | bytes 786440 | tf_op jit(solution)/shard_map/ppermute | solution.py:36
  37.8 13.8 %all-to-all-start.2 = ((bf16[8,32,1024]{2,1,0:T(8,128)(2,1)}), bf16[8,32,1024]{2,1,0:T(8,128)(2,1)S(1)}, u32[]{:S(2)}, u32[]{:S(2)}) async-start(bf16[8,32,1024]{2,1,0:T(8,128)(2,1)} %attend.1), calls=%async_computation.2 | async-start | bytes 1048576 | tf_op jit(solution)/shard_map/all_to_all | solution.py:52
  52.6 1.6 %collective-permute-start.4 = (bf16[128,1024]{1,0:T(8,128)(2,1)S(1)}, bf16[128,1024]{1,0:T(8,128)(2,1)S(1)}, u32[]{:S(2)}, u32[]{:S(2)}) collective-permute-start(bf16[128,1024]{1,0:T(8,128)(2,1)S(1)} %output.3), channel_id=1, source_target_pairs={{0,8},{1,9},{2,10},{3,11},{4,12},{5,13},{6,14},{7,15},{8,0},{9,1},... | collective-permute-start | bytes 786440 | tf_op jit(solution)/shard_map/ppermute | solution.py:36
  64.2 7.3 %collective-permute-start.5 = (bf16[4,4,1024]{2,1,0:T(4,128)(2,1)S(1)}, bf16[4,4,1024]{2,1,0:T(4,128)(2,1)S(1)}, u32[]{:S(2)}, u32[]{:S(2)}) collective-permute-start(bf16[4,4,1024]{2,1,0:T(4,128)(2,1)S(1)} %reshape.226), channel_id=1, source_target_pairs={{0,32},{1,16},{2,0},{3,48},{4,96},{5,80},{6,64},{7,112},{8,40},{9,... | collective-permute-start | bytes 98312 | tf_op jit(solution)/shard_map/ppermute | solution.py:36
